TPU v7x, 256 devices: a whole 4x4x8 slice. The times are simulated.
256 devices in a mesh: dp: 256 (over y, z, x, core).
Axes of the slice: x: 4, y: 4, z: 8, core: 2. Of those that a mesh axis runs over, the one named last changes fastest.
Arguments:
- picture_vectors: bfloat16 [98304, 1152], P('dp'), may hold values from -6 to 6
- caption_vectors: bfloat16 [98304, 1152], P('dp'), may hold values from -6 to 6
- photo_couple_tags: int32 [98304], P('dp'), may hold values from 0 to 3071
- caption_match_ids: int32 [98304], P('dp'), may hold values from 0 to 3071
- affinity_stretch: float32 [1], replicated, may hold values from 2 to 4
- score_offset: float32 [1], replicated, may hold values from -3 to -1
Outputs:
- loss_rows: float32 [98304], P('dp')
- image_unit_gradient: float32 [98304, 1152], P('dp')
- text_unit_gradient: float32 [98304, 1152], P('dp')
All inputs are finite; a program needn't handle non-finite values.
Results may differ from a plain program's by a relative error of at most 0.0039.
Values may be sent and summed in bfloat16 or wider, within the bound.
A program may use at most 64 MiB of HBM per device.

v0:
```python
import jax
import jax.numpy as jnp
from jax import lax
from jax.sharding import PartitionSpec as P

REACH = 3


def shifted(value, axis, steps):
    count = lax.axis_size(axis)
    pairs = [(source, (source + steps) % count) for source in range(count)]
    return lax.ppermute(value, axis, pairs)


def unit_rows(value_entries):
    broadened = value_entries.astype(jnp.float32)
    reciprocal_warmth_gain = lax.rsqrt(
        jnp.sum(broadened * broadened, axis=-1, keepdims=True) + 1e-06
    )
    return (broadened * reciprocal_warmth_gain).astype(jnp.bfloat16)


def tile_weighting(
    local_portion,
    local_embedding_tiles,
    visiting_portion,
    visiting_embedding_tiles,
    reciprocal_warmth_gain,
    displacement,
):
    raw_affinity = (
        reciprocal_warmth_gain
        * jnp.dot(local_portion, visiting_portion.T, preferred_element_type=jnp.float32)
        + displacement
    )
    target_sign = jnp.where(
        local_embedding_tiles[:, None] == visiting_embedding_tiles[None, :], 1.0, -1.0
    ).astype(jnp.float32)
    weighting_term = (
        -target_sign * jax.nn.sigmoid(-target_sign * raw_affinity) * reciprocal_warmth_gain
    ).astype(jnp.bfloat16)
    return (raw_affinity, target_sign, weighting_term)


def affinity_tile(
    local_portion,
    local_embedding_tiles,
    visiting_portion,
    visiting_embedding_tiles,
    reciprocal_warmth_gain,
    displacement,
):
    raw_affinity, target_sign, weighting_term = tile_weighting(
        local_portion,
        local_embedding_tiles,
        visiting_portion,
        visiting_embedding_tiles,
        reciprocal_warmth_gain,
        displacement,
    )
    loss_part = jnp.sum(jax.nn.softplus(-target_sign * raw_affinity), axis=1)
    image_part = jnp.dot(weighting_term, visiting_portion, preferred_element_type=jnp.float32)
    text_part = lax.dot_general(
        weighting_term, local_portion, (((0,), (0,)), ((), ())), preferred_element_type=jnp.float32
    )
    return (loss_part, image_part, text_part)


def shards(
    picture_vectors,
    caption_vectors,
    photo_couple_tags,
    caption_match_ids,
    affinity_stretch,
    score_offset,
):
    local_portion = unit_rows(picture_vectors)
    partner_own = unit_rows(caption_vectors)
    reciprocal_warmth_gain = affinity_stretch[0]
    displacement = score_offset[0]
    loss_sum, image_unit_gradient, text_unit_gradient = affinity_tile(
        local_portion,
        photo_couple_tags,
        partner_own,
        caption_match_ids,
        reciprocal_warmth_gain,
        displacement,
    )
    for sign in (1, -1):
        travelling = (partner_own, caption_match_ids)
        carried = None
        for step in range(REACH):
            travelling = shifted((travelling[0], travelling[1]), "dp", sign)
            if carried is not None:
                carried = shifted(carried, "dp", sign)
            loss_part, image_part, text_part = affinity_tile(
                local_portion,
                photo_couple_tags,
                travelling[0],
                travelling[1],
                reciprocal_warmth_gain,
                displacement,
            )
            loss_sum = loss_sum + loss_part
            image_unit_gradient = image_unit_gradient + image_part
            carried = text_part if carried is None else carried + text_part
        text_unit_gradient = text_unit_gradient + shifted(carried, "dp", -sign * REACH)
    loss_rows = loss_sum / ((2 * REACH + 1) * local_portion.shape[0])
    return (loss_rows, image_unit_gradient, text_unit_gradient)


def solution(mesh):
    placed = (P("dp", None), P("dp", None), P("dp"), P("dp"), P(), P())
    return jax.shard_map(
        shards,
        mesh=mesh,
        in_specs=placed,
        out_specs=(P("dp"), P("dp", None), P("dp", None)),
        check_vma=False,
    )
```

profile of v0, /device:TPU:248, one launch (start us, length us, event | category | flops | bytes accessed | tf_op | source)
XLA Modules:
  0.0 182.2 jit_solution(14842367510158360502)
XLA Ops:
  0.7 1.5 fusion.3
  2.2 1.4 fusion.4
  3.6 2.7 %collective-permute-start.7 = (bf16[384,1152]{1,0:T(8,128)(2,1)S(1)}, bf16[384,1152]{1,0:T(8,128)(2,1)S(1)}, u32[]{:S(2)}, u32[]{:S(2)}) collective-permute-start(bf16[384,1152]{1,0:T(8,128)(2,1)S(1)} %fusion.4), channel_id=1, source_target_pairs={{0,255},{1,0},{2,1},{3,2},{4,3},{5,4},{6,5},{7,6},{8,7},{9,8},{10,... | collective-permute-start | bytes 2654216 | tf_op jit(solution)/shard_map/ppermute | solution.py:12
  8.5 8.3 %collective-permute-done.6 = s32[384]{0:T(512)S(1)} collective-permute-done((s32[384]{0:T(512)S(1)}, s32[384]{0:T(512)S(1)}, u32[]{:S(2)}, u32[]{:S(2)}) %collective-permute-start.6) | collective-permute-done | bytes 1568 | tf_op jit(solution)/shard_map/ppermute | solution.py:12
  16.9 1.1 fusion.23
  18.8 4.1 %collective-permute-start.15 = (f32[384,1152]{1,0:T(8,128)S(1)}, f32[384,1152]{1,0:T(8,128)S(1)}, u32[]{:S(2)}, u32[]{:S(2)}) collective-permute-start(f32[384,1152]{1,0:T(8,128)S(1)} %fusion.31), channel_id=1, source_target_pairs={{0,255},{1,0},{2,1},{3,2},{4,3},{5,4},{6,5},{7,6},{8,7},{9,8},{10,... | collective-permute-start | bytes 5308424 | tf_op jit(solution)/shard_map/ppermute | solution.py:12
  23.0 1.1 fusion.20
  25.5 3.8 %collective-permute-start.8 = (s32[384]{0:T(512)S(1)}, s32[384]{0:T(512)S(1)}, u32[]{:S(2)}, u32[]{:S(2)}) collective-permute-start(s32[384]{0:T(512)S(1)} %collective-permute-done.6), channel_id=1, source_target_pairs={{0,255},{1,0},{2,1},{3,2},{4,3},{5,4},{6,5},{7,6},{8,7},{9,8},{10,... | collective-permute-start | bytes 4616 | tf_op jit(solution)/shard_map/ppermute | solution.py:12
  29.3 1.1 fusion.19
  30.4 22.0 %collective-permute-done.8 = s32[384]{0:T(512)S(1)} collective-permute-done((s32[384]{0:T(512)S(1)}, s32[384]{0:T(512)S(1)}, u32[]{:S(2)}, u32[]{:S(2)}) %collective-permute-start.8) | collective-permute-done | bytes 1568 | tf_op jit(solution)/shard_map/ppermute | solution.py:12
  52.5 4.0 %collective-permute-start.11 = (bf16[384,1152]{1,0:T(8,128)(2,1)S(1)}, bf16[384,1152]{1,0:T(8,128)(2,1)S(1)}, u32[]{:S(2)}, u32[]{:S(2)}) collective-permute-start(bf16[384,1152]{1,0:T(8,128)(2,1)S(1)} %collective-permute-done.9), channel_id=1, source_target_pairs={{0,255},{1,0},{2,1},{3,2},{4,3},{5,4},{6,5},{7,6},{8,7},{9,8},{10,... | collective-permute-start | bytes 2654216 | tf_op jit(solution)/shard_map/ppermute | solution.py:12
  56.5 1.1 fusion.24
  57.6 1.0 collective-permute-done.2
  58.6 1.1 fusion.21
  63.9 3.9 %collective-permute-start.10 = (s32[384]{0:T(512)S(1)}, s32[384]{0:T(512)S(1)}, u32[]{:S(2)}, u32[]{:S(2)}) collective-permute-start(s32[384]{0:T(512)S(1)} %collective-permute-done.8), channel_id=1, source_target_pairs={{0,255},{1,0},{2,1},{3,2},{4,3},{5,4},{6,5},{7,6},{8,7},{9,8},{10,... | collective-permute-start | bytes 4616 | tf_op jit(solution)/shard_map/ppermute | solution.py:12
  68.6 17.4 %collective-permute-done.10 = s32[384]{0:T(512)S(1)} collective-permute-done((s32[384]{0:T(512)S(1)}, s32[384]{0:T(512)S(1)}, u32[]{:S(2)}, u32[]{:S(2)}) %collective-permute-start.10) | collective-permute-done | bytes 1568 | tf_op jit(solution)/shard_map/ppermute | solution.py:12
  86.0 1.1 fusion.25
  87.1 8.0 %collective-permute-done.4 = s32[384]{0:T(512)S(1)} collective-permute-done((s32[384]{0:T(512)S(1)}, s32[384]{0:T(512)S(1)}, u32[]{:S(2)}, u32[]{:S(2)}) %collective-permute-start.4) | collective-permute-done | bytes 1568 | tf_op jit(solution)/shard_map/ppermute | solution.py:12
  95.2 1.1 fusion.22
  98.1 4.2 %collective-permute-start.14 = (f32[384,1152]{1,0:T(8,128)S(1)}, f32[384,1152]{1,0:T(8,128)S(1)}, u32[]{:S(2)}, u32[]{:S(2)}) collective-permute-start(f32[384,1152]{1,0:T(8,128)S(1)} %fusion.30), channel_id=1, source_target_pairs={{0,253},{1,254},{2,255},{3,0},{4,1},{5,2},{6,3},{7,4},{8,5},{9,6},... | collective-permute-start | bytes 5308424 | tf_op jit(solution)/shard_map/ppermute | solution.py:12
  106.2 2.0 %convolution_add_fusion.2 = f32[384,1152]{1,0:T(8,128)} fusion(f32[384,1152]{1,0:T(8,128)S(1)} %convolution_add_fusion.3, bf16[384,1152]{1,0:T(8,128)(2,1)S(1)} %collective-permute-done.11, f32[384,384]{0,1:T(8,128)S(1)} %get-tuple-element.4, f32[]{:T(128)} %bitcast.17, s32[384]{0:T(512)S(1)} %copy-done.1, s32[384]{0:T(512)S(1)} %collective-permute-done.10), kind=kOutput, calls=%fused_computation.2 | convolution fusion | flops 341508096 | bytes 5016580 | tf_op jit(solution)/shard_map/dot_general | solution.py:62
  108.2 46.7 %collective-permute-done.17 = f32[384,1152]{1,0:T(8,128)S(1)} collective-permute-done((f32[384,1152]{1,0:T(8,128)S(1)}, f32[384,1152]{1,0:T(8,128)S(1)}, u32[]{:S(2)}, u32[]{:S(2)}) %collective-permute-start.17) | collective-permute-done | bytes 1769504 | tf_op jit(solution)/shard_map/ppermute | solution.py:12
  154.9 25.8 %collective-permute-done.14 = f32[384,1152]{1,0:T(8,128)S(1)} collective-permute-done((f32[384,1152]{1,0:T(8,128)S(1)}, f32[384,1152]{1,0:T(8,128)S(1)}, u32[]{:S(2)}, u32[]{:S(2)}) %collective-permute-start.14) | collective-permute-done | bytes 1769504 | tf_op jit(solution)/shard_map/ppermute | solution.py:12
  180.7 1.5 add_add_fusion
  (46 shorter events, 13.9 us)
Async XLA Ops:
  0.6 5.6 %copy-start.2 = (s32[384]{0:T(512)S(1)}, s32[384]{0:T(512)}, u32[]{:S(2)}) copy-start(s32[384]{0:T(512)} %param.9) | copy-start | bytes 4612
  0.6 6.3 %copy-start = (bf16[384,1152]{1,0:T(8,128)(2,1)S(1)}, bf16[384,1152]{1,0:T(8,128)(2,1)}, u32[]{:S(2)}) copy-start(bf16[384,1152]{1,0:T(8,128)(2,1)} %param.6) | copy-start | bytes 2654212
  0.7 16.2 %copy-start.1 = (s32[384]{0:T(512)S(1)}, s32[384]{0:T(512)}, u32[]{:S(2)}) copy-start(s32[384]{0:T(512)} %param.8) | copy-start | bytes 4612
  3.6 13.3 %collective-permute-start.7 = (bf16[384,1152]{1,0:T(8,128)(2,1)S(1)}, bf16[384,1152]{1,0:T(8,128)(2,1)S(1)}, u32[]{:S(2)}, u32[]{:S(2)}) collective-permute-start(bf16[384,1152]{1,0:T(8,128)(2,1)S(1)} %fusion.4), channel_id=1, source_target_pairs={{0,255},{1,0},{2,1},{3,2},{4,3},{5,4},{6,5},{7,6},{8,7},{9,8},{10,... | collective-permute-start | bytes 2654216 | tf_op jit(solution)/shard_map/ppermute | solution.py:12
  6.3 10.6 %collective-permute-start.6 = (s32[384]{0:T(512)S(1)}, s32[384]{0:T(512)S(1)}, u32[]{:S(2)}, u32[]{:S(2)}) collective-permute-start(s32[384]{0:T(512)S(1)} %copy-done.2), channel_id=1, source_target_pairs={{0,255},{1,0},{2,1},{3,2},{4,3},{5,4},{6,5},{7,6},{8,7},{9,8},{10,... | collective-permute-start | bytes 4616 | tf_op jit(solution)/shard_map/ppermute | solution.py:12
  7.0 16.0 %collective-permute-start = (s32[384]{0:T(512)S(1)}, s32[384]{0:T(512)S(1)}, u32[]{:S(2)}, u32[]{:S(2)}) collective-permute-start(s32[384]{0:T(512)S(1)} %copy-done.2), channel_id=1, source_target_pairs={{0,1},{1,2},{2,3},{3,4},{4,5},{5,6},{6,7},{7,8},{8,9},{9,10},{10,1... | collective-permute-start | bytes 4616 | tf_op jit(solution)/shard_map/ppermute | solution.py:12
  7.0 16.0 %collective-permute-start.1 = (bf16[384,1152]{1,0:T(8,128)(2,1)S(1)}, bf16[384,1152]{1,0:T(8,128)(2,1)S(1)}, u32[]{:S(2)}, u32[]{:S(2)}) collective-permute-start(bf16[384,1152]{1,0:T(8,128)(2,1)S(1)} %fusion.4), channel_id=1, source_target_pairs={{0,1},{1,2},{2,3},{3,4},{4,5},{5,6},{6,7},{7,8},{8,9},{9,10},{10,1... | collective-permute-start | bytes 2654216 | tf_op jit(solution)/shard_map/ppermute | solution.py:12
  18.8 40.9 %collective-permute-start.15 = (f32[384,1152]{1,0:T(8,128)S(1)}, f32[384,1152]{1,0:T(8,128)S(1)}, u32[]{:S(2)}, u32[]{:S(2)}) collective-permute-start(f32[384,1152]{1,0:T(8,128)S(1)} %fusion.31), channel_id=1, source_target_pairs={{0,255},{1,0},{2,1},{3,2},{4,3},{5,4},{6,5},{7,6},{8,7},{9,8},{10,... | collective-permute-start | bytes 5308424 | tf_op jit(solution)/shard_map/ppermute | solution.py:12
  22.9 29.6 %collective-permute-start.9 = (bf16[384,1152]{1,0:T(8,128)(2,1)S(1)}, bf16[384,1152]{1,0:T(8,128)(2,1)S(1)}, u32[]{:S(2)}, u32[]{:S(2)}) collective-permute-start(bf16[384,1152]{1,0:T(8,128)(2,1)S(1)} %collective-permute-done.7), channel_id=1, source_target_pairs={{0,255},{1,0},{2,1},{3,2},{4,3},{5,4},{6,5},{7,6},{8,7},{9,8},{10,... | collective-permute-start | bytes 2654216 | tf_op jit(solution)/shard_map/ppermute | solution.py:12
  25.0 35.7 %collective-permute-start.12 = (f32[384,1152]{1,0:T(8,128)S(1)}, f32[384,1152]{1,0:T(8,128)S(1)}, u32[]{:S(2)}, u32[]{:S(2)}) collective-permute-start(f32[384,1152]{1,0:T(8,128)S(1)} %fusion.28), channel_id=1, source_target_pairs={{0,1},{1,2},{2,3},{3,4},{4,5},{5,6},{6,7},{7,8},{8,9},{9,10},{10,1... | collective-permute-start | bytes 5308424 | tf_op jit(solution)/shard_map/ppermute | solution.py:12
  25.5 33.1 %collective-permute-start.3 = (bf16[384,1152]{1,0:T(8,128)(2,1)S(1)}, bf16[384,1152]{1,0:T(8,128)(2,1)S(1)}, u32[]{:S(2)}, u32[]{:S(2)}) collective-permute-start(bf16[384,1152]{1,0:T(8,128)(2,1)S(1)} %collective-permute-done.1), channel_id=1, source_target_pairs={{0,1},{1,2},{2,3},{3,4},{4,5},{5,6},{6,7},{7,8},{8,9},{9,10},{10,1... | collective-permute-start | bytes 2654216 | tf_op jit(solution)/shard_map/ppermute | solution.py:12
  25.5 26.9 %collective-permute-start.8 = (s32[384]{0:T(512)S(1)}, s32[384]{0:T(512)S(1)}, u32[]{:S(2)}, u32[]{:S(2)}) collective-permute-start(s32[384]{0:T(512)S(1)} %collective-permute-done.6), channel_id=1, source_target_pairs={{0,255},{1,0},{2,1},{3,2},{4,3},{5,4},{6,5},{7,6},{8,7},{9,8},{10,... | collective-permute-start | bytes 4616 | tf_op jit(solution)/shard_map/ppermute | solution.py:12
  52.5 6.1 %collective-permute-start.2 = (s32[384]{0:T(512)S(1)}, s32[384]{0:T(512)S(1)}, u32[]{:S(2)}, u32[]{:S(2)}) collective-permute-start(s32[384]{0:T(512)S(1)} %collective-permute-done), channel_id=1, source_target_pairs={{0,1},{1,2},{2,3},{3,4},{4,5},{5,6},{6,7},{7,8},{8,9},{9,10},{10,1... | collective-permute-start | bytes 4616 | tf_op jit(solution)/shard_map/ppermute | solution.py:12
  52.5 33.6 %collective-permute-start.11 = (bf16[384,1152]{1,0:T(8,128)(2,1)S(1)}, bf16[384,1152]{1,0:T(8,128)(2,1)S(1)}, u32[]{:S(2)}, u32[]{:S(2)}) collective-permute-start(bf16[384,1152]{1,0:T(8,128)(2,1)S(1)} %collective-permute-done.9), channel_id=1, source_target_pairs={{0,255},{1,0},{2,1},{3,2},{4,3},{5,4},{6,5},{7,6},{8,7},{9,8},{10,... | collective-permute-start | bytes 2654216 | tf_op jit(solution)/shard_map/ppermute | solution.py:12
  60.6 35.7 %collective-permute-start.16 = (f32[384,1152]{1,0:T(8,128)S(1)}, f32[384,1152]{1,0:T(8,128)S(1)}, u32[]{:S(2)}, u32[]{:S(2)}) collective-permute-start(f32[384,1152]{1,0:T(8,128)S(1)} %convolution_add_fusion), channel_id=1, source_target_pairs={{0,255},{1,0},{2,1},{3,2},{4,3},{5,4},{6,5},{7,6},{8,7},{9,8},{10,... | collective-permute-start | bytes 5308424 | tf_op jit(solution)/shard_map/ppermute | solution.py:12
  61.5 35.7 %collective-permute-start.13 = (f32[384,1152]{1,0:T(8,128)S(1)}, f32[384,1152]{1,0:T(8,128)S(1)}, u32[]{:S(2)}, u32[]{:S(2)}) collective-permute-start(f32[384,1152]{1,0:T(8,128)S(1)} %convolution_add_fusion.1), channel_id=1, source_target_pairs={{0,1},{1,2},{2,3},{3,4},{4,5},{5,6},{6,7},{7,8},{8,9},{9,10},{10,1... | collective-permute-start | bytes 5308424 | tf_op jit(solution)/shard_map/ppermute | solution.py:12
  63.0 32.2 %collective-permute-start.5 = (bf16[384,1152]{1,0:T(8,128)(2,1)S(1)}, bf16[384,1152]{1,0:T(8,128)(2,1)S(1)}, u32[]{:S(2)}, u32[]{:S(2)}) collective-permute-start(bf16[384,1152]{1,0:T(8,128)(2,1)S(1)} %collective-permute-done.3), channel_id=1, source_target_pairs={{0,1},{1,2},{2,3},{3,4},{4,5},{5,6},{6,7},{7,8},{8,9},{9,10},{10,1... | collective-permute-start | bytes 2654216 | tf_op jit(solution)/shard_map/ppermute | solution.py:12
  63.9 22.1 %collective-permute-start.10 = (s32[384]{0:T(512)S(1)}, s32[384]{0:T(512)S(1)}, u32[]{:S(2)}, u32[]{:S(2)}) collective-permute-start(s32[384]{0:T(512)S(1)} %collective-permute-done.8), channel_id=1, source_target_pairs={{0,255},{1,0},{2,1},{3,2},{4,3},{5,4},{6,5},{7,6},{8,7},{9,8},{10,... | collective-permute-start | bytes 4616 | tf_op jit(solution)/shard_map/ppermute | solution.py:12
  86.0 9.2 %collective-permute-start.4 = (s32[384]{0:T(512)S(1)}, s32[384]{0:T(512)S(1)}, u32[]{:S(2)}, u32[]{:S(2)}) collective-permute-start(s32[384]{0:T(512)S(1)} %collective-permute-done.2), channel_id=1, source_target_pairs={{0,1},{1,2},{2,3},{3,4},{4,5},{5,6},{6,7},{7,8},{8,9},{9,10},{10,1... | collective-permute-start | bytes 4616 | tf_op jit(solution)/shard_map/ppermute | solution.py:12
  97.2 57.8 %collective-permute-start.17 = (f32[384,1152]{1,0:T(8,128)S(1)}, f32[384,1152]{1,0:T(8,128)S(1)}, u32[]{:S(2)}, u32[]{:S(2)}) collective-permute-start(f32[384,1152]{1,0:T(8,128)S(1)} %fusion.34), channel_id=1, source_target_pairs={{0,3},{1,4},{2,5},{3,6},{4,7},{5,8},{6,9},{7,10},{8,11},{9,12},{10... | collective-permute-start | bytes 5308424 | tf_op jit(solution)/shard_map/ppermute | solution.py:12
  98.1 82.6 %collective-permute-start.14 = (f32[384,1152]{1,0:T(8,128)S(1)}, f32[384,1152]{1,0:T(8,128)S(1)}, u32[]{:S(2)}, u32[]{:S(2)}) collective-permute-start(f32[384,1152]{1,0:T(8,128)S(1)} %fusion.30), channel_id=1, source_target_pairs={{0,253},{1,254},{2,255},{3,0},{4,1},{5,2},{6,3},{7,4},{8,5},{9,6},... | collective-permute-start | bytes 5308424 | tf_op jit(solution)/shard_map/ppermute | solution.py:12
where the time goes:
time: 182 us
  waiting for transfers between devices  129 us (71%)
  starting transfers between devices  24.9 us (14%)
  matrix products  20.5 us (11%)
  other arithmetic  5.2 us (3%)
  between operations  2.11 us (1%)
    ppermute x18, waiting for transfers between devices, shifted(): return lax.ppermute(value, axis, pairs)  129 us
    ppermute x18, starting transfers between devices, shifted(): return lax.ppermute(value, axis, pairs)  24.9 us
    dot_general x7, matrix products, tile_weighting(): jnp.dot(local_portion, visiting_portion.T, preferred_element_type=jnp.flo...  7.69 us
    dot_general x7, matrix products, affinity_tile(): jnp.dot(weighting_term, visiting_portion, preferred_element_type=jnp.floa...  6.82 us
    dot_general x7, matrix products, affinity_tile(): lax.dot_general(weighting_term, local_portion, (((0,), (0,)), ((), ())),...  6 us
  transfers between devices with their start and end apart: 18, of which 7 were waited for; matrix products, arithmetic and copies ran while one was open for 12% of the time, Pallas kernels for 0%

commit v1 on v0

v1 whole, which is shorter than its diff:
```python
import math

import jax
import jax.numpy as jnp
from jax import lax
from jax.experimental import pallas as pl
from jax.experimental.pallas import tpu as pltpu
from jax.sharding import PartitionSpec as P

MESH = pl.DeviceIdType.MESH
REACH = 3
ROWS = 128
OUT1, IN3, IN2, OUT2, IN1, OUT3 = range(6)
TEXT, IMAGE = 0, 1


def kernel(
    stretch_ref,
    offset_ref,
    picture_ref,
    caption_ref,
    couple_ref,
    match_ref,
    loss_ref,
    image_grad_ref,
    text_grad_ref,
    raw,
    own,
    held,
    own_tags,
    tags,
    columns,
    load_sem,
    send_sem,
    recv_sem,
    tag_send_sem,
    tag_recv_sem,
):
    count = lax.axis_size("dp")
    me = lax.axis_index("dp")
    sign = 2 * lax.rem(me, 2) - 1
    pieces = own.shape[1]

    def at(steps):
        return lax.rem(me + steps * sign + count, count)

    target = {OUT1: at(1), IN3: at(-3), IN2: at(-1), OUT2: at(-1), IN1: at(-1), OUT3: at(-2)}

    barrier = pltpu.get_barrier_semaphore()
    for steps in (1, -3, -1, 2):
        pl.semaphore_signal(barrier, inc=1, device_id=(at(steps),), device_id_type=MESH)

    def load(side, piece):
        source = (caption_ref, picture_ref)[side]
        return pltpu.make_async_copy(
            source.at[pl.ds(piece * ROWS, ROWS)], raw.at[side, piece], load_sem.at[side, piece]
        )

    for piece in range(pieces):
        for side in (TEXT, IMAGE):
            load(side, piece).start()

    half = 0.5 * stretch_ref[0]
    shift = 0.5 * offset_ref[0]

    def normalize(side, piece):
        load(side, piece).wait()
        value = raw[side, piece].astype(jnp.float32)
        gain = lax.rsqrt(jnp.sum(value * value, axis=-1, keepdims=True) + 1e-06)
        own[side, piece] = (value * gain).astype(jnp.bfloat16)

    def source_of(slot, side, piece):
        if slot in (OUT1, IN3, IN1):
            return own.at[side, piece]
        return held.at[side, piece, IN3 if slot == OUT2 else OUT1]

    def send(slot, side, piece):
        return pltpu.make_async_remote_copy(
            src_ref=source_of(slot, side, piece),
            dst_ref=held.at[side, piece, slot],
            send_sem=send_sem.at[slot, side, piece],
            recv_sem=recv_sem.at[slot, side, piece],
            device_id=(target[slot],),
            device_id_type=MESH,
        )

    def send_tags(slot):
        if slot in (OUT1, IN3, IN1):
            source = own_tags
        else:
            source = tags.at[IN3 if slot == OUT2 else OUT1]
        return pltpu.make_async_remote_copy(
            src_ref=source,
            dst_ref=tags.at[slot],
            send_sem=tag_send_sem.at[slot],
            recv_sem=tag_recv_sem.at[slot],
            device_id=(target[slot],),
            device_id_type=MESH,
        )

    own_tags[TEXT : TEXT + 1, :] = match_ref[...]
    own_tags[IMAGE : IMAGE + 1, :] = couple_ref[...]
    own_tags[2:8, :] = jnp.zeros((6, own_tags.shape[1]), jnp.int32)
    normalize(TEXT, 0)
    normalize(IMAGE, 0)
    pl.semaphore_wait(barrier, 4)
    for slot in (OUT1, IN3, IN1):
        send_tags(slot).start()
    for piece in range(pieces):
        if piece:
            normalize(TEXT, piece)
            normalize(IMAGE, piece)
        for side in (TEXT, IMAGE):
            for slot in (OUT1, IN3, IN1):
                send(slot, side, piece).start()

    for side, source in ((TEXT, couple_ref), (IMAGE, match_ref)):
        for piece in range(pieces):
            row = source[0:1, piece * ROWS : (piece + 1) * ROWS]
            columns[side, piece * ROWS : (piece + 1) * ROWS, :] = jnp.broadcast_to(
                row, (128, ROWS)
            ).T

    loss_ref[...] = jnp.zeros_like(loss_ref)

    def unit(side, block, row, first=False):
        mine = own[1 - side].reshape(-1, block.shape[1])
        total_ref = (image_grad_ref, text_grad_ref)[side]
        product = lax.dot_general(
            mine, block, (((1,), (1,)), ((), ())), preferred_element_type=jnp.float32
        )
        bend = jnp.tanh(half * product + shift)
        groups = block.shape[0] // 128
        equal = jnp.concatenate([columns[side]] * groups, axis=1) == row
        coef = (half * bend + jnp.where(equal, -half, half)).astype(jnp.bfloat16)
        if side == TEXT:
            kept = 1.0 - jnp.where(equal, -bend, bend)
            wide = kept[:, :128]
            for group in range(1, groups):
                wide = wide * kept[:, group * 128 : (group + 1) * 128]
            loss_ref[...] += jnp.log(wide)
        part = jnp.dot(coef, block, preferred_element_type=jnp.float32)
        if first:
            total_ref[...] = part
        else:
            total_ref[...] += part

    def slot_tags(side, piece, slots):
        span = pl.ds(pl.multiple_of(piece * ROWS, ROWS), ROWS)
        return jnp.concatenate([tags[slot, side : side + 1, span] for slot in slots], axis=1)

    def slot_unit(side, piece, low, high):
        block = held[side, piece, low : high + 1].reshape(-1, held.shape[-1])
        unit(side, block, slot_tags(side, piece, range(low, high + 1)))

    for side in (TEXT, IMAGE):
        block = own[side].reshape(-1, own.shape[-1])
        unit(side, block, own_tags[side : side + 1, :], first=True)

    send_tags(IN1).wait_recv()
    for side in (TEXT, IMAGE):

        def near_body(piece, carry, side=side):
            send(IN1, side, piece).wait_recv()
            slot_unit(side, piece, IN1, IN1)
            return carry

        lax.fori_loop(0, pieces, near_body, 0)

    send_tags(OUT1).wait_recv()
    send_tags(IN2).start()
    send_tags(OUT3).start()
    send_tags(IN3).wait_recv()
    send_tags(OUT2).start()
    send_tags(IN2).wait_recv()
    send_tags(OUT2).wait_recv()
    send_tags(OUT3).wait_recv()

    def body(piece, carry):
        for side in (TEXT, IMAGE):
            send(OUT1, side, piece).wait_recv()
            send(IN2, side, piece).start()
            send(OUT3, side, piece).start()
            send(IN3, side, piece).wait_recv()
            send(OUT2, side, piece).start()
        for side in (TEXT, IMAGE):
            slot_unit(side, piece, OUT1, IN3)
        for side in (TEXT, IMAGE):
            send(IN2, side, piece).wait_recv()
            send(OUT2, side, piece).wait_recv()
            slot_unit(side, piece, IN2, OUT2)
        return carry

    lax.fori_loop(0, pieces, body, 0)

    def last_body(piece, carry):
        for side in (TEXT, IMAGE):
            send(OUT3, side, piece).wait_recv()
            slot_unit(side, piece, OUT3, OUT3)
        return carry

    lax.fori_loop(0, pieces, last_body, 0)

    for slot in range(6):
        send_tags(slot).wait_send()

        def drain(piece, carry, slot=slot):
            for side in (TEXT, IMAGE):
                send(slot, side, piece).wait_send()
            return carry

        lax.fori_loop(0, pieces, drain, 0)


def shards(
    picture_vectors,
    caption_vectors,
    photo_couple_tags,
    caption_match_ids,
    affinity_stretch,
    score_offset,
):
    rows, width = picture_vectors.shape
    pieces = rows // ROWS
    vmem = pl.BlockSpec(memory_space=pltpu.VMEM)
    smem = pl.BlockSpec(memory_space=pltpu.SMEM)
    anywhere = pl.BlockSpec(memory_space=pl.ANY)
    loss_parts, image_unit_gradient, text_unit_gradient = pl.pallas_call(
        kernel,
        out_shape=(
            jax.ShapeDtypeStruct((rows, 128), jnp.float32),
            jax.ShapeDtypeStruct((rows, width), jnp.float32),
            jax.ShapeDtypeStruct((rows, width), jnp.float32),
        ),
        in_specs=[smem, smem, anywhere, anywhere, vmem, vmem],
        out_specs=(vmem, vmem, vmem),
        scratch_shapes=[
            pltpu.VMEM((2, pieces, ROWS, width), jnp.bfloat16),
            pltpu.VMEM((2, pieces, ROWS, width), jnp.bfloat16),
            pltpu.VMEM((2, pieces, 6, ROWS, width), jnp.bfloat16),
            pltpu.VMEM((8, rows), jnp.int32),
            pltpu.VMEM((6, 8, rows), jnp.int32),
            pltpu.VMEM((2, rows, 128), jnp.int32),
            pltpu.SemaphoreType.DMA((2, pieces)),
            pltpu.SemaphoreType.DMA((6, 2, pieces)),
            pltpu.SemaphoreType.DMA((6, 2, pieces)),
            pltpu.SemaphoreType.DMA((6,)),
            pltpu.SemaphoreType.DMA((6,)),
        ],
        compiler_params=pltpu.CompilerParams(
            collective_id=0, has_side_effects=True, vmem_limit_bytes=40 * 1024 * 1024
        ),
        name="window_loss",
    )(
        affinity_stretch,
        score_offset,
        picture_vectors,
        caption_vectors,
        photo_couple_tags.reshape(1, rows),
        caption_match_ids.reshape(1, rows),
    )
    loss_rows = math.log(2.0) - jnp.sum(loss_parts, axis=1) / ((2 * REACH + 1) * rows)
    return (loss_rows, image_unit_gradient, text_unit_gradient)


def solution(mesh):
    placed = (P("dp", None), P("dp", None), P("dp"), P("dp"), P(), P())
    return jax.shard_map(
        shards,
        mesh=mesh,
        in_specs=placed,
        out_specs=(P("dp"), P("dp", None), P("dp", None)),
        check_vma=False,
    )
```

time: 182 us -> 86.2 us (0.47)
  the two profiles are of different devices: /device:TPU:248 before, /device:TPU:0 now
where the time goes in v1:
time: 86.2 us; the launch traced here: 86 us
  Pallas kernels  75.6 us (88%)
  local copies, waits for them, and re-layouts  6.78 us (8%)
  between operations  1.94 us (2%)
  other arithmetic  1.66 us (2%)
    pallas_call x1, Pallas kernels, shards(): pl.pallas_call(kernel, out_shape=(jax.ShapeDtypeStruct((rows, 128), jnp.f...  75.6 us
    unnamed x8, local copies, waits for them, and re-layouts  5.42 us

profile of v1, /device:TPU:0, one launch (start us, length us, event | category | flops | bytes accessed | tf_op | source)
XLA Modules:
  0.0 86.0 jit_solution(1351439132415681522)
XLA Ops:
  1.9 0.7 reshape.12.couple_ref
  2.6 0.7 reshape.13.match_ref
  3.3 0.0 copy-start
  3.3 1.2 %copy-done = bf16[384,1152]{1,0:T(8,128)(2,1)S(1)} copy-done((bf16[384,1152]{1,0:T(8,128)(2,1)S(1)}, bf16[384,1152]{1,0:T(8,128)(2,1)}, u32[]{:S(2)}) %copy-start) | copy-done | bytes 884760
  4.5 0.0 copy-start.1
  4.5 1.2 %copy-done.1 = bf16[384,1152]{1,0:T(8,128)(2,1)S(1)} copy-done((bf16[384,1152]{1,0:T(8,128)(2,1)S(1)}, bf16[384,1152]{1,0:T(8,128)(2,1)}, u32[]{:S(2)}) %copy-start.1) | copy-done | bytes 884760
  5.6 75.6 %window_loss.1 = (f32[384,128]{1,0:T(8,128)S(1)}, f32[384,1152]{1,0:T(8,128)S(1)}, f32[384,1152]{1,0:T(8,128)S(1)}) custom-call(f32[1]{0:T(128)S(6)} %copy.11.stretch_ref, f32[1]{0:T(128)S(6)} %copy.12.offset_ref, bf16[384,1152]{1,0:T(8,128)(2,1)S(1)} %copy-done, bf16[384,1152]{1,0:T(8,128)(2,1)S(1)} %copy-done.1, s32[1,384]{1,0:T(1,128)S(1)} %reshape.12.couple_ref, ...), custom_call_target="tpu_custom_call" | custom-call | tf_op jit(solution)/shard_map/window_loss/pallas_call | solution.py:228
  81.2 0.0 copy-start.2
  81.2 0.7 copy-done.2
  81.9 1.1 %reduce_sum.9 = f32[384]{0:T(512)S(1)} reduce(f32[384,128]{1,0:T(8,128)} %copy-done.2, f32[]{:T(128)} %constant.2.clone.1), dimensions={1}, to_apply=%region_0.0 | reduce | flops 48768 | bytes 198148 | tf_op jit(solution)/shard_map/reduce_sum | solution.py:262
  82.9 0.6 multiply_subtract_fusion
  83.5 1.2 %copy.13 = f32[384,1152]{1,0:T(8,128)} copy(f32[384,1152]{1,0:T(8,128)S(1)} %get-tuple-element.13) | data formatting | bytes 3538944
  84.7 1.2 %copy.14 = f32[384,1152]{1,0:T(8,128)} copy(f32[384,1152]{1,0:T(8,128)S(1)} %get-tuple-element.14) | data formatting | bytes 3538944
Async XLA Ops:
  3.3 1.2 %copy-start = (bf16[384,1152]{1,0:T(8,128)(2,1)S(1)}, bf16[384,1152]{1,0:T(8,128)(2,1)}, u32[]{:S(2)}) copy-start(bf16[384,1152]{1,0:T(8,128)(2,1)} %picture_ref.1) | copy-start | bytes 2654212
  4.5 1.2 %copy-start.1 = (bf16[384,1152]{1,0:T(8,128)(2,1)S(1)}, bf16[384,1152]{1,0:T(8,128)(2,1)}, u32[]{:S(2)}) copy-start(bf16[384,1152]{1,0:T(8,128)(2,1)} %caption_ref.1) | copy-start | bytes 2654212
  81.2 0.7 copy-start.2

commit v2 on v1

--- a/solution.py
+++ b/solution.py
@@ -15,8 +15,8 @@
 
 
 def kernel(
-    stretch_ref,
-    offset_ref,
+    stretch_hbm,
+    offset_hbm,
     picture_ref,
     caption_ref,
     couple_ref,
@@ -27,10 +27,14 @@
     raw,
     own,
     held,
+    stretch_ref,
+    offset_ref,
+    flat_tags,
     own_tags,
     tags,
     columns,
     load_sem,
+    tag_load_sem,
     send_sem,
     recv_sem,
     tag_send_sem,
@@ -56,12 +60,22 @@
             source.at[pl.ds(piece * ROWS, ROWS)], raw.at[side, piece], load_sem.at[side, piece]
         )
 
+    def load_tags(side):
+        source = (match_ref, couple_ref)[side]
+        return pltpu.make_async_copy(source, flat_tags[side], tag_load_sem.at[side])
+
     for piece in range(pieces):
         for side in (TEXT, IMAGE):
             load(side, piece).start()
-
-    half = 0.5 * stretch_ref[0]
-    shift = 0.5 * offset_ref[0]
+            if piece == 0:
+                load_tags(side).start()
+
+    scalars = (
+        pltpu.make_async_copy(stretch_hbm, stretch_ref, tag_load_sem.at[2]),
+        pltpu.make_async_copy(offset_hbm, offset_ref, tag_load_sem.at[3]),
+    )
+    for copy in scalars:
+        copy.start()
 
     def normalize(side, piece):
         load(side, piece).wait()
@@ -98,8 +112,10 @@
             device_id_type=MESH,
         )
 
-    own_tags[TEXT : TEXT + 1, :] = match_ref[...]
-    own_tags[IMAGE : IMAGE + 1, :] = couple_ref[...]
+    rows = own_tags.shape[1]
+    for side in (TEXT, IMAGE):
+        load_tags(side).wait()
+        own_tags[side : side + 1, :] = flat_tags[side][...].reshape(1, rows)
     own_tags[2:8, :] = jnp.zeros((6, own_tags.shape[1]), jnp.int32)
     normalize(TEXT, 0)
     normalize(IMAGE, 0)
@@ -111,16 +127,22 @@
             normalize(TEXT, piece)
             normalize(IMAGE, piece)
         for side in (TEXT, IMAGE):
-            for slot in (OUT1, IN3, IN1):
-                send(slot, side, piece).start()
-
-    for side, source in ((TEXT, couple_ref), (IMAGE, match_ref)):
+            send(OUT1, side, piece).start()
+            if piece == 0:
+                send(IN3, side, piece).start()
+            send(IN1, side, piece).start()
+
+    for side in (TEXT, IMAGE):
         for piece in range(pieces):
-            row = source[0:1, piece * ROWS : (piece + 1) * ROWS]
+            row = own_tags[1 - side : 2 - side, piece * ROWS : (piece + 1) * ROWS]
             columns[side, piece * ROWS : (piece + 1) * ROWS, :] = jnp.broadcast_to(
                 row, (128, ROWS)
             ).T
 
+    for copy in scalars:
+        copy.wait()
+    half = 0.5 * stretch_ref[0]
+    shift = 0.5 * offset_ref[0]
     loss_ref[...] = jnp.zeros_like(loss_ref)
 
     def unit(side, block, row, first=False):
@@ -158,14 +180,15 @@
         unit(side, block, own_tags[side : side + 1, :], first=True)
 
     send_tags(IN1).wait_recv()
-    for side in (TEXT, IMAGE):
-
-        def near_body(piece, carry, side=side):
+
+    def near_body(piece, carry):
+        for side in (TEXT, IMAGE):
             send(IN1, side, piece).wait_recv()
+        for side in (TEXT, IMAGE):
             slot_unit(side, piece, IN1, IN1)
-            return carry
-
-        lax.fori_loop(0, pieces, near_body, 0)
+        return carry
+
+    lax.fori_loop(0, pieces, near_body, 0)
 
     send_tags(OUT1).wait_recv()
     send_tags(IN2).start()
@@ -176,11 +199,22 @@
     send_tags(OUT2).wait_recv()
     send_tags(OUT3).wait_recv()
 
+    def last_piece(piece):
+        for side in (TEXT, IMAGE):
+            send(OUT3, side, piece).wait_recv()
+        for side in (TEXT, IMAGE):
+            slot_unit(side, piece, OUT3, OUT3)
+
     def body(piece, carry):
         for side in (TEXT, IMAGE):
             send(OUT1, side, piece).wait_recv()
             send(IN2, side, piece).start()
             send(OUT3, side, piece).start()
+
+            @pl.when(piece + 1 < pieces)
+            def _(side=side):
+                send(IN3, side, piece + 1).start()
+
             send(IN3, side, piece).wait_recv()
             send(OUT2, side, piece).start()
         for side in (TEXT, IMAGE):
@@ -188,18 +222,18 @@
         for side in (TEXT, IMAGE):
             send(IN2, side, piece).wait_recv()
             send(OUT2, side, piece).wait_recv()
+        for side in (TEXT, IMAGE):
             slot_unit(side, piece, IN2, OUT2)
+
+        @pl.when(piece > 0)
+        def _():
+            last_piece(piece - 1)
+
         return carry
 
     lax.fori_loop(0, pieces, body, 0)
 
-    def last_body(piece, carry):
-        for side in (TEXT, IMAGE):
-            send(OUT3, side, piece).wait_recv()
-            slot_unit(side, piece, OUT3, OUT3)
-        return carry
-
-    lax.fori_loop(0, pieces, last_body, 0)
+    last_piece(pieces - 1)
 
     for slot in range(6):
         send_tags(slot).wait_send()
@@ -210,6 +244,32 @@
             return carry
 
         lax.fori_loop(0, pieces, drain, 0)
+
+
+def finish(loss_ref, image_grad_ref, text_grad_ref, loss_out, image_out, text_out, sem):
+    rows, lanes = loss_ref.shape
+    copies = []
+    for piece in range(rows // ROWS):
+        span = pl.ds(piece * ROWS, ROWS)
+        for side, (source, target) in enumerate(
+            ((text_grad_ref, text_out), (image_grad_ref, image_out))
+        ):
+            copies.append(
+                pltpu.make_async_copy(source.at[span], target.at[span], sem.at[side, piece])
+            )
+    for copy in copies:
+        copy.start()
+    sums = lax.dot_general(
+        jnp.ones((8, lanes), jnp.float32),
+        loss_ref[...],
+        (((1,), (1,)), ((), ())),
+        precision=lax.Precision.HIGHEST,
+        preferred_element_type=jnp.float32,
+    )
+    loss = math.log(2.0) - sums[0:1] / ((2 * REACH + 1) * rows)
+    loss_out[...] = loss.reshape(rows)
+    for copy in copies:
+        copy.wait()
 
 
 def shards(
@@ -222,26 +282,37 @@
 ):
     rows, width = picture_vectors.shape
     pieces = rows // ROWS
+    operands = (
+        affinity_stretch,
+        score_offset,
+        picture_vectors,
+        caption_vectors,
+        photo_couple_tags,
+        caption_match_ids,
+    )
     vmem = pl.BlockSpec(memory_space=pltpu.VMEM)
-    smem = pl.BlockSpec(memory_space=pltpu.SMEM)
-    anywhere = pl.BlockSpec(memory_space=pl.ANY)
+    hbm = pl.BlockSpec(memory_space=pltpu.HBM)
     loss_parts, image_unit_gradient, text_unit_gradient = pl.pallas_call(
         kernel,
         out_shape=(
-            jax.ShapeDtypeStruct((rows, 128), jnp.float32),
-            jax.ShapeDtypeStruct((rows, width), jnp.float32),
-            jax.ShapeDtypeStruct((rows, width), jnp.float32),
+            pltpu.VMEM((rows, 128), jnp.float32),
+            pltpu.VMEM((rows, width), jnp.float32),
+            pltpu.VMEM((rows, width), jnp.float32),
         ),
-        in_specs=[smem, smem, anywhere, anywhere, vmem, vmem],
+        in_specs=[hbm] * 6,
         out_specs=(vmem, vmem, vmem),
         scratch_shapes=[
             pltpu.VMEM((2, pieces, ROWS, width), jnp.bfloat16),
             pltpu.VMEM((2, pieces, ROWS, width), jnp.bfloat16),
             pltpu.VMEM((2, pieces, 6, ROWS, width), jnp.bfloat16),
+            pltpu.SMEM((1,), jnp.float32),
+            pltpu.SMEM((1,), jnp.float32),
+            [pltpu.VMEM((rows,), jnp.int32)] * 2,
             pltpu.VMEM((8, rows), jnp.int32),
             pltpu.VMEM((6, 8, rows), jnp.int32),
             pltpu.VMEM((2, rows, 128), jnp.int32),
             pltpu.SemaphoreType.DMA((2, pieces)),
+            pltpu.SemaphoreType.DMA((4,)),
             pltpu.SemaphoreType.DMA((6, 2, pieces)),
             pltpu.SemaphoreType.DMA((6, 2, pieces)),
             pltpu.SemaphoreType.DMA((6,)),
@@ -252,15 +323,24 @@
         ),
         name="window_loss",
     )(
-        affinity_stretch,
-        score_offset,
-        picture_vectors,
-        caption_vectors,
-        photo_couple_tags.reshape(1, rows),
-        caption_match_ids.reshape(1, rows),
-    )
-    loss_rows = math.log(2.0) - jnp.sum(loss_parts, axis=1) / ((2 * REACH + 1) * rows)
-    return (loss_rows, image_unit_gradient, text_unit_gradient)
+        *(
+            pltpu.with_memory_space_constraint(array, pltpu.HBM) if array.size > 1 else array
+            for array in operands
+        )
+    )
+    return pl.pallas_call(
+        finish,
+        out_shape=(
+            jax.ShapeDtypeStruct((rows,), jnp.float32),
+            jax.ShapeDtypeStruct((rows, width), jnp.float32),
+            jax.ShapeDtypeStruct((rows, width), jnp.float32),
+        ),
+        in_specs=[vmem, vmem, vmem],
+        out_specs=(vmem, hbm, hbm),
+        scratch_shapes=[pltpu.SemaphoreType.DMA((2, pieces))],
+        compiler_params=pltpu.CompilerParams(vmem_limit_bytes=8 * 1024 * 1024),
+        name="write_out",
+    )(loss_parts, image_unit_gradient, text_unit_gradient)
 
 
 def solution(mesh):

time: 86.2 us -> 77.1 us (0.89)
  the two profiles are of different devices: /device:TPU:0 before, /device:TPU:2 now
where the time goes in v2:
time: 77.1 us; the launch traced here: 76.3 us
  Pallas kernels  74.4 us (96%)
  between operations  1.93 us (3%)
    pallas_call x1, Pallas kernels, shards(): pl.pallas_call(kernel, out_shape=(pltpu.VMEM((rows, 128), jnp.float32), p...  72 us
    pallas_call x1, Pallas kernels, shards(): pl.pallas_call(finish, out_shape=(jax.ShapeDtypeStruct((rows,), jnp.float...  2.41 us

profile of v2, /device:TPU:2, one launch (start us, length us, event | category | flops | bytes accessed | tf_op | source)
XLA Modules:
  0.0 76.3 jit_solution(12185506709908486667)
XLA Ops:
  1.9 72.0 %window_loss.1 = (f32[384,128]{1,0:T(8,128)S(1)}, f32[384,1152]{1,0:T(8,128)S(1)}, f32[384,1152]{1,0:T(8,128)S(1)}) custom-call(f32[1]{0:T(128)S(6)} %copy.9.stretch_hbm, f32[1]{0:T(128)S(6)} %copy.10.offset_hbm, bf16[384,1152]{1,0:T(8,128)(2,1)} %picture_ref.1, bf16[384,1152]{1,0:T(8,128)(2,1)} %caption_ref.1, s32[384]{0:T(512)} %couple_ref.1, s32[384]{0:T(512)} %match_ref.1), custom_call_target="tpu_custom_call" | custom-call | tf_op jit(solution)/shard_map/window_loss/pallas_call | solution.py:295
  73.9 2.4 %write_out.1 = (f32[384]{0:T(512)}, f32[384,1152]{1,0:T(8,128)}, f32[384,1152]{1,0:T(8,128)}) custom-call(f32[384,128]{1,0:T(8,128)S(1)} %get-tuple-element.6.loss_ref, f32[384,1152]{1,0:T(8,128)S(1)} %get-tuple-element.7.image_grad_ref, f32[384,1152]{1,0:T(8,128)S(1)} %get-tuple-element.8.text_grad_ref), custom_call_target="tpu_custom_call" | custom-call | tf_op jit(solution)/shard_map/write_out/pallas_call | solution.py:331

commit v3 on v2

--- a/solution.py
+++ b/solution.py
@@ -10,6 +10,7 @@
 MESH = pl.DeviceIdType.MESH
 REACH = 3
 ROWS = 128
+LEAD = 2
 OUT1, IN3, IN2, OUT2, IN1, OUT3 = range(6)
 TEXT, IMAGE = 0, 1
 
@@ -24,6 +25,8 @@
     loss_ref,
     image_grad_ref,
     text_grad_ref,
+    coef_ref,
+    block_ref,
     raw,
     own,
     held,
@@ -64,12 +67,11 @@
         source = (match_ref, couple_ref)[side]
         return pltpu.make_async_copy(source, flat_tags[side], tag_load_sem.at[side])
 
-    for piece in range(pieces):
-        for side in (TEXT, IMAGE):
+    for side in (TEXT, IMAGE):
+        load_tags(side).start()
+    for side in (TEXT, IMAGE):
+        for piece in range(pieces):
             load(side, piece).start()
-            if piece == 0:
-                load_tags(side).start()
-
     scalars = (
         pltpu.make_async_copy(stretch_hbm, stretch_ref, tag_load_sem.at[2]),
         pltpu.make_async_copy(offset_hbm, offset_ref, tag_load_sem.at[3]),
@@ -118,17 +120,15 @@
         own_tags[side : side + 1, :] = flat_tags[side][...].reshape(1, rows)
     own_tags[2:8, :] = jnp.zeros((6, own_tags.shape[1]), jnp.int32)
     normalize(TEXT, 0)
-    normalize(IMAGE, 0)
     pl.semaphore_wait(barrier, 4)
     for slot in (OUT1, IN3, IN1):
         send_tags(slot).start()
-    for piece in range(pieces):
-        if piece:
-            normalize(TEXT, piece)
-            normalize(IMAGE, piece)
-        for side in (TEXT, IMAGE):
+    for side in (TEXT, IMAGE):
+        for piece in range(pieces):
+            if piece or side:
+                normalize(side, piece)
             send(OUT1, side, piece).start()
-            if piece == 0:
+            if side == TEXT and piece < LEAD:
                 send(IN3, side, piece).start()
             send(IN1, side, piece).start()
 
@@ -145,20 +145,22 @@
     shift = 0.5 * offset_ref[0]
     loss_ref[...] = jnp.zeros_like(loss_ref)
 
-    def unit(side, block, row, first=False):
+    def weigh(side, block, row):
         mine = own[1 - side].reshape(-1, block.shape[1])
-        total_ref = (image_grad_ref, text_grad_ref)[side]
         product = lax.dot_general(
             mine, block, (((1,), (1,)), ((), ())), preferred_element_type=jnp.float32
         )
         bend = jnp.tanh(half * product + shift)
-        groups = block.shape[0] // 128
-        equal = jnp.concatenate([columns[side]] * groups, axis=1) == row
-        coef = (half * bend + jnp.where(equal, -half, half)).astype(jnp.bfloat16)
+        equal = jnp.concatenate([columns[side]] * (block.shape[0] // 128), axis=1) == row
+        coef = half * bend + jnp.where(equal, -half, half)
+        return coef.astype(jnp.bfloat16), 1.0 - jnp.where(equal, -bend, bend)
+
+    def unit(side, block, row, first=False):
+        total_ref = (image_grad_ref, text_grad_ref)[side]
+        coef, kept = weigh(side, block, row)
         if side == TEXT:
-            kept = 1.0 - jnp.where(equal, -bend, bend)
             wide = kept[:, :128]
-            for group in range(1, groups):
+            for group in range(1, block.shape[0] // 128):
                 wide = wide * kept[:, group * 128 : (group + 1) * 128]
             loss_ref[...] += jnp.log(wide)
         part = jnp.dot(coef, block, preferred_element_type=jnp.float32)
@@ -199,41 +201,52 @@
     send_tags(OUT2).wait_recv()
     send_tags(OUT3).wait_recv()
 
-    def last_piece(piece):
-        for side in (TEXT, IMAGE):
-            send(OUT3, side, piece).wait_recv()
-        for side in (TEXT, IMAGE):
-            slot_unit(side, piece, OUT3, OUT3)
-
-    def body(piece, carry):
-        for side in (TEXT, IMAGE):
+    def relayed(side, piece):
+        send(OUT3, side, piece).wait_recv()
+        slot_unit(side, piece, OUT3, OUT3)
+
+    for side in (TEXT, IMAGE):
+
+        def body(piece, carry, side=side):
             send(OUT1, side, piece).wait_recv()
             send(IN2, side, piece).start()
             send(OUT3, side, piece).start()
 
-            @pl.when(piece + 1 < pieces)
-            def _(side=side):
-                send(IN3, side, piece + 1).start()
+            @pl.when(piece + LEAD < pieces)
+            def _():
+                send(IN3, side, piece + LEAD).start()
+
+            if side == TEXT:
+
+                @pl.when(piece + LEAD >= pieces)
+                def _():
+                    send(IN3, IMAGE, piece + LEAD - pieces).start()
 
             send(IN3, side, piece).wait_recv()
             send(OUT2, side, piece).start()
-        for side in (TEXT, IMAGE):
             slot_unit(side, piece, OUT1, IN3)
-        for side in (TEXT, IMAGE):
             send(IN2, side, piece).wait_recv()
             send(OUT2, side, piece).wait_recv()
-        for side in (TEXT, IMAGE):
             slot_unit(side, piece, IN2, OUT2)
 
-        @pl.when(piece > 0)
-        def _():
-            last_piece(piece - 1)
-
-        return carry
-
-    lax.fori_loop(0, pieces, body, 0)
-
-    last_piece(pieces - 1)
+            @pl.when(piece > 0)
+            def _():
+                relayed(side, piece - 1)
+
+            if side == IMAGE:
+
+                @pl.when(piece == 0)
+                def _():
+                    relayed(TEXT, pieces - 1)
+
+            return carry
+
+        lax.fori_loop(0, pieces, body, 0)
+
+    send(OUT3, IMAGE, pieces - 1).wait_recv()
+    block = held[IMAGE, pieces - 1, OUT3]
+    coef_ref[...] = weigh(IMAGE, block, slot_tags(IMAGE, pieces - 1, [OUT3]))[0]
+    block_ref[...] = block
 
     for slot in range(6):
         send_tags(slot).wait_send()
@@ -246,19 +259,27 @@
         lax.fori_loop(0, pieces, drain, 0)
 
 
-def finish(loss_ref, image_grad_ref, text_grad_ref, loss_out, image_out, text_out, sem):
+def finish(
+    loss_ref, image_grad_ref, text_grad_ref, coef_ref, block_ref, loss_out, image_out, text_out, total, sem
+):
     rows, lanes = loss_ref.shape
     copies = []
+
+    def write(side, piece):
+        span = pl.ds(piece * ROWS, ROWS)
+        source, target = ((total, text_out), (image_grad_ref, image_out))[side]
+        copy = pltpu.make_async_copy(source.at[span], target.at[span], sem.at[side, piece])
+        copy.start()
+        copies.append(copy)
+
+    for piece in range(rows // ROWS):
+        write(IMAGE, piece)
     for piece in range(rows // ROWS):
         span = pl.ds(piece * ROWS, ROWS)
-        for side, (source, target) in enumerate(
-            ((text_grad_ref, text_out), (image_grad_ref, image_out))
-        ):
-            copies.append(
-                pltpu.make_async_copy(source.at[span], target.at[span], sem.at[side, piece])
-            )
-    for copy in copies:
-        copy.start()
+        total[span] = text_grad_ref[span] + jnp.dot(
+            coef_ref[span], block_ref[...], preferred_element_type=jnp.float32
+        )
+        write(TEXT, piece)
     sums = lax.dot_general(
         jnp.ones((8, lanes), jnp.float32),
         loss_ref[...],
@@ -292,15 +313,17 @@
     )
     vmem = pl.BlockSpec(memory_space=pltpu.VMEM)
     hbm = pl.BlockSpec(memory_space=pltpu.HBM)
-    loss_parts, image_unit_gradient, text_unit_gradient = pl.pallas_call(
+    parts = pl.pallas_call(
         kernel,
         out_shape=(
             pltpu.VMEM((rows, 128), jnp.float32),
             pltpu.VMEM((rows, width), jnp.float32),
             pltpu.VMEM((rows, width), jnp.float32),
+            pltpu.VMEM((rows, ROWS), jnp.bfloat16),
+            pltpu.VMEM((ROWS, width), jnp.bfloat16),
         ),
         in_specs=[hbm] * 6,
-        out_specs=(vmem, vmem, vmem),
+        out_specs=(vmem,) * 5,
         scratch_shapes=[
             pltpu.VMEM((2, pieces, ROWS, width), jnp.bfloat16),
             pltpu.VMEM((2, pieces, ROWS, width), jnp.bfloat16),
@@ -335,12 +358,12 @@
             jax.ShapeDtypeStruct((rows, width), jnp.float32),
             jax.ShapeDtypeStruct((rows, width), jnp.float32),
         ),
-        in_specs=[vmem, vmem, vmem],
+        in_specs=[vmem] * 5,
         out_specs=(vmem, hbm, hbm),
-        scratch_shapes=[pltpu.SemaphoreType.DMA((2, pieces))],
+        scratch_shapes=[pltpu.VMEM((rows, width), jnp.float32), pltpu.SemaphoreType.DMA((2, pieces))],
         compiler_params=pltpu.CompilerParams(vmem_limit_bytes=8 * 1024 * 1024),
         name="write_out",
-    )(loss_parts, image_unit_gradient, text_unit_gradient)
+    )(*parts)
 
 
 def solution(mesh):

time: 77.1 us -> 76 us (0.986)
  Pallas kernels: 74.4 us -> 73.3 us
    pallas_call x1, Pallas kernels: 72 us -> 70.8 us  [shards(): pl.pallas_call(kernel, out_shape=(pltpu.VMEM((rows, 128), jnp.float32), p...]
where the time goes in v3:
time: 76 us; the launch traced here: 75.2 us
  Pallas kernels  73.3 us (96%)
  between operations  1.93 us (3%)
    pallas_call x1, Pallas kernels, shards(): pl.pallas_call(kernel, out_shape=(pltpu.VMEM((rows, 128), jnp.float32), p...  70.8 us
    pallas_call x1, Pallas kernels, shards(): pl.pallas_call(finish, out_shape=(jax.ShapeDtypeStruct((rows,), jnp.float...  2.47 us

profile of v3, /device:TPU:2, one launch (start us, length us, event | category | flops | bytes accessed | tf_op | source)
XLA Modules:
  0.0 75.2 jit_solution(13336670691526858225)
XLA Ops:
  1.9 70.8 %window_loss.1 = (f32[384,128]{1,0:T(8,128)S(1)}, f32[384,1152]{1,0:T(8,128)S(1)}, f32[384,1152]{1,0:T(8,128)S(1)}, bf16[384,128]{1,0:T(8,128)(2,1)S(1)}, bf16[128,1152]{1,0:T(8,128)(2,1)S(1)}) custom-call(f32[1]{0:T(128)S(6)} %copy.9.stretch_hbm, f32[1]{0:T(128)S(6)} %copy.10.offset_hbm, bf16[384,1152]{1,0:T(8,128)(2,1)} %picture_ref.1, ...), custom_call_target="tpu_custom_call" | custom-call | tf_op jit(solution)/shard_map/window_loss/pallas_call | solution.py:316
  72.8 2.5 %write_out.1 = (f32[384]{0:T(512)}, f32[384,1152]{1,0:T(8,128)}, f32[384,1152]{1,0:T(8,128)}) custom-call(f32[384,128]{1,0:T(8,128)S(1)} %get-tuple-element.8.loss_ref, f32[384,1152]{1,0:T(8,128)S(1)} %get-tuple-element.9.image_grad_ref, f32[384,1152]{1,0:T(8,128)S(1)} %get-tuple-element.10.text_grad_ref, bf16[384,128]{1,0:T(8,128)(2,1)S(1)} %get-tuple-element.11.coef_ref, ...), custom_call_target="tpu_custom_call" | custom-call | tf_op jit(solution)/shard_map/write_out/pallas_call | solution.py:354

commit v4 on v3

--- a/solution.py
+++ b/solution.py
@@ -205,43 +205,59 @@
         send(OUT3, side, piece).wait_recv()
         slot_unit(side, piece, OUT3, OUT3)
 
+    def pass_on(side, piece):
+        send(OUT1, side, piece).wait_recv()
+        send(OUT3, side, piece).start()
+        send(IN2, side, piece).start()
+
+        @pl.when(piece + LEAD < pieces)
+        def _():
+            send(IN3, side, piece + LEAD).start()
+
+        if side == TEXT:
+
+            @pl.when(piece + LEAD >= pieces)
+            def _():
+                send(IN3, IMAGE, piece + LEAD - pieces).start()
+
+    def work(side, piece):
+        send(IN3, side, piece).wait_recv()
+        send(OUT2, side, piece).start()
+        slot_unit(side, piece, OUT1, IN3)
+        send(IN2, side, piece).wait_recv()
+        send(OUT2, side, piece).wait_recv()
+        slot_unit(side, piece, IN2, OUT2)
+
     for side in (TEXT, IMAGE):
 
         def body(piece, carry, side=side):
-            send(OUT1, side, piece).wait_recv()
-            send(IN2, side, piece).start()
-            send(OUT3, side, piece).start()
-
-            @pl.when(piece + LEAD < pieces)
-            def _():
-                send(IN3, side, piece + LEAD).start()
-
-            if side == TEXT:
-
-                @pl.when(piece + LEAD >= pieces)
-                def _():
-                    send(IN3, IMAGE, piece + LEAD - pieces).start()
-
-            send(IN3, side, piece).wait_recv()
-            send(OUT2, side, piece).start()
-            slot_unit(side, piece, OUT1, IN3)
-            send(IN2, side, piece).wait_recv()
-            send(OUT2, side, piece).wait_recv()
-            slot_unit(side, piece, IN2, OUT2)
+            pass_on(side, piece)
 
             @pl.when(piece > 0)
             def _():
-                relayed(side, piece - 1)
+                work(side, piece - 1)
+
+            @pl.when(piece > 1)
+            def _():
+                relayed(side, piece - 2)
 
             if side == IMAGE:
 
                 @pl.when(piece == 0)
                 def _():
+                    work(TEXT, pieces - 1)
+                    relayed(TEXT, pieces - 2)
+
+                @pl.when(piece == 1)
+                def _():
                     relayed(TEXT, pieces - 1)
 
             return carry
 
         lax.fori_loop(0, pieces, body, 0)
+
+    work(IMAGE, pieces - 1)
+    relayed(IMAGE, pieces - 2)
 
     send(OUT3, IMAGE, pieces - 1).wait_recv()
     block = held[IMAGE, pieces - 1, OUT3]

time: 76 us -> 75.7 us (level)
  no operation moved by 1% of the time
where the time goes in v4:
time: 75.7 us; the launch traced here: 75.6 us
  Pallas kernels  73.5 us (97%)
  between operations  2.09 us (3%)
    pallas_call x1, Pallas kernels, shards(): pl.pallas_call(kernel, out_shape=(pltpu.VMEM((rows, 128), jnp.float32), p...  71 us
    pallas_call x1, Pallas kernels, shards(): pl.pallas_call(finish, out_shape=(jax.ShapeDtypeStruct((rows,), jnp.float...  2.47 us

profile of v4, /device:TPU:2, one launch (start us, length us, event | category | flops | bytes accessed | tf_op | source)
XLA Modules:
  0.0 75.6 jit_solution(8228297067008589441)
XLA Ops:
  1.9 71.0 %window_loss.1 = (f32[384,128]{1,0:T(8,128)S(1)}, f32[384,1152]{1,0:T(8,128)S(1)}, f32[384,1152]{1,0:T(8,128)S(1)}, bf16[384,128]{1,0:T(8,128)(2,1)S(1)}, bf16[128,1152]{1,0:T(8,128)(2,1)S(1)}) custom-call(f32[1]{0:T(128)S(6)} %copy.9.stretch_hbm, f32[1]{0:T(128)S(6)} %copy.10.offset_hbm, bf16[384,1152]{1,0:T(8,128)(2,1)} %picture_ref.1, ...), custom_call_target="tpu_custom_call" | custom-call | tf_op jit(solution)/shard_map/window_loss/pallas_call | solution.py:332
  73.0 2.5 %write_out.1 = (f32[384]{0:T(512)}, f32[384,1152]{1,0:T(8,128)}, f32[384,1152]{1,0:T(8,128)}) custom-call(f32[384,128]{1,0:T(8,128)S(1)} %get-tuple-element.8.loss_ref, f32[384,1152]{1,0:T(8,128)S(1)} %get-tuple-element.9.image_grad_ref, f32[384,1152]{1,0:T(8,128)S(1)} %get-tuple-element.10.text_grad_ref, bf16[384,128]{1,0:T(8,128)(2,1)S(1)} %get-tuple-element.11.coef_ref, ...), custom_call_target="tpu_custom_call" | custom-call | tf_op jit(solution)/shard_map/write_out/pallas_call | solution.py:370

commit v5 on v4

--- a/solution.py
+++ b/solution.py
@@ -130,6 +130,8 @@
             send(OUT1, side, piece).start()
             if side == TEXT and piece < LEAD:
                 send(IN3, side, piece).start()
+    for side in (TEXT, IMAGE):
+        for piece in range(pieces):
             send(IN1, side, piece).start()
 
     for side in (TEXT, IMAGE):

time: 75.7 us -> 75.7 us (level)
  no operation moved by 1% of the time
where the time goes in v5:
time: 75.7 us; the launch traced here: 75.6 us
  Pallas kernels  73.5 us (97%)
  between operations  2.09 us (3%)
    pallas_call x1, Pallas kernels, shards(): pl.pallas_call(kernel, out_shape=(pltpu.VMEM((rows, 128), jnp.float32), p...  71 us
    pallas_call x1, Pallas kernels, shards(): pl.pallas_call(finish, out_shape=(jax.ShapeDtypeStruct((rows,), jnp.float...  2.47 us

profile of v5, /device:TPU:2, one launch (start us, length us, event | category | flops | bytes accessed | tf_op | source)
XLA Modules:
  0.0 75.6 jit_solution(14619196290724402107)
XLA Ops:
  1.9 71.0 %window_loss.1 = (f32[384,128]{1,0:T(8,128)S(1)}, f32[384,1152]{1,0:T(8,128)S(1)}, f32[384,1152]{1,0:T(8,128)S(1)}, bf16[384,128]{1,0:T(8,128)(2,1)S(1)}, bf16[128,1152]{1,0:T(8,128)(2,1)S(1)}) custom-call(f32[1]{0:T(128)S(6)} %copy.9.stretch_hbm, f32[1]{0:T(128)S(6)} %copy.10.offset_hbm, bf16[384,1152]{1,0:T(8,128)(2,1)} %picture_ref.1, ...), custom_call_target="tpu_custom_call" | custom-call | tf_op jit(solution)/shard_map/window_loss/pallas_call | solution.py:334
  73.0 2.5 %write_out.1 = (f32[384]{0:T(512)}, f32[384,1152]{1,0:T(8,128)}, f32[384,1152]{1,0:T(8,128)}) custom-call(f32[384,128]{1,0:T(8,128)S(1)} %get-tuple-element.8.loss_ref, f32[384,1152]{1,0:T(8,128)S(1)} %get-tuple-element.9.image_grad_ref, f32[384,1152]{1,0:T(8,128)S(1)} %get-tuple-element.10.text_grad_ref, bf16[384,128]{1,0:T(8,128)(2,1)S(1)} %get-tuple-element.11.coef_ref, ...), custom_call_target="tpu_custom_call" | custom-call | tf_op jit(solution)/shard_map/write_out/pallas_call | solution.py:372
